TPU v7x, 512 devices: a whole 4x4x16 slice. The times are simulated.
512 devices in a mesh: ctx: 32 (over x, z_hi, core), resp: 16 (over z_lo, y).
Axes of the slice: x: 4, y: 4, z: 16 (z_hi: 4, z_lo: 4; z = z_hi * 4 + z_lo), core: 2. Of those that a mesh axis runs over, the one named last changes fastest.
Arguments:
- queries: bfloat16 [16, 4096, 4096], P('resp', 'ctx'), may hold values from -96 to 96
- attention_output: bfloat16 [16, 4096, 4096], P('resp', 'ctx'), may hold values from -6 to 6
- grad_out: bfloat16 [16, 4096, 4096], P('resp', 'ctx'), may hold values from -6 to 6
- own_log_sum_exp: float32 [16, 4096, 32], P('resp', 'ctx'), may hold values from 2 to 9
- prompt_keys: bfloat16 [512, 512], P('ctx'), may hold values from -6 to 6
- prompt_value_rows: bfloat16 [512, 512], P('ctx'), may hold values from -6 to 6
- advantages: float32 [16], P('resp'), may hold values from -3 to 3
- lengths: int32 [16], P('resp'), may hold values from 1024 to 4096, as said below
- mamba_in: bfloat16 [512, 8192], P('ctx', 'resp'), may hold values from -6 to 6
- step_size: float32 [512, 8192], P('ctx', 'resp'), may hold values from 0 to 0.2
- decay_rate: float32 [16, 8192], P(None, 'resp'), may hold values from 0.25 to 4
- input_map: float32 [512, 16], P('ctx'), may hold values from -6 to 6
- output_map: float32 [512, 16], P('ctx'), may hold values from -6 to 6
- mamba_grad: bfloat16 [512, 8192], P('ctx', 'resp'), may hold values from -6 to 6
- state_grad: bfloat16 [16, 16, 8192], P('resp'), may hold values from -24 to 24
Outputs:
- query_grad: bfloat16 [16, 4096, 4096], P('resp', 'ctx')
- key_grad: float32 [512, 512], P('ctx')
- value_grad: float32 [512, 512], P('ctx')
- mamba_input_grad: float32 [512, 8192], P('ctx', 'resp')
- input_map_grad: float32 [512, 16], P('ctx')
Inputs may be any that keep to these rules, and one draw needn't show every extreme that they name: `lengths`: some response fills all 4096 positions and some other response has 1024 tokens.
All inputs are finite; a program needn't handle non-finite values.
Results may differ from a plain program's by a relative error of at most 0.02.
Values may be sent and summed in bfloat16 or wider, within the bound.
A program may use at most 64 MiB of HBM per device.

v0:
```python
import math

import jax
import jax.numpy as jnp
from jax import lax
from jax.sharding import PartitionSpec as P

QUERY_HEADS = 32
KEY_VALUE_HEADS = 4
HEAD_SIZE = 128


def carried_in(part, axis, combine, identity):
    count = lax.axis_size(axis)
    place = lax.axis_index(axis)
    ahead = count - 1 - place
    gathered = jax.tree.map(lambda a: lax.all_gather(a, axis), part)
    state = jax.tree.map(lambda a, e: jnp.zeros_like(a) + jnp.asarray(e, a.dtype), part, identity)

    def one(turn, state):
        source = count - 1 - turn
        return combine(
            state, jax.tree.map(lambda a: lax.dynamic_index_in_dim(a, source, 0, False), gathered)
        )

    return lax.fori_loop(0, ahead, one, state)


def contract_last(left, right):
    return lax.dot_general(
        left, right, (((1,), (1,)), ((), ())), preferred_element_type=jnp.float32
    )


def contract_first(left, right):
    return lax.dot_general(
        left, right, (((0,), (0,)), ((), ())), preferred_element_type=jnp.float32
    )


def prefix_terms(query_rows, grad_rows, output_rows, own_rows, keys_head, values_head, score_scale):
    scores = contract_last(query_rows, keys_head) * score_scale
    row_max = jnp.max(scores, axis=1)
    prefix_lse = row_max + jnp.log(jnp.sum(jnp.exp(scores - row_max[:, None]), axis=1))
    larger = jnp.maximum(prefix_lse, own_rows)
    total_lse = larger + jnp.log(jnp.exp(prefix_lse - larger) + jnp.exp(own_rows - larger))
    prob_rows = jnp.exp(scores - total_lse[:, None])
    row_inner = jnp.sum(grad_rows.astype(jnp.float32) * output_rows.astype(jnp.float32), axis=1)
    dprob_rows = contract_last(grad_rows, values_head)
    dscores = (prob_rows * (dprob_rows - row_inner[:, None])).astype(jnp.bfloat16)
    return (prob_rows.astype(jnp.bfloat16), dscores)


def compose_maps(earlier, later):
    return (later[0] * earlier[0], later[0] * earlier[1] + later[1])


def on_device(
    queries,
    attention_output,
    grad_out,
    own_log_sum_exp,
    prompt_keys,
    prompt_value_rows,
    advantages,
    lengths,
    mamba_in,
    step_size,
    decay_rate,
    input_map,
    output_map,
    mamba_grad,
    state_grad,
):
    token_count = queries.shape[1]
    query_group_width = QUERY_HEADS // KEY_VALUE_HEADS
    score_scale = 1.0 / math.sqrt(HEAD_SIZE)
    total_len = token_count * lax.axis_size("ctx")
    position = lax.axis_index("ctx") * token_count + jnp.arange(token_count, dtype=jnp.int32)
    weight = advantages * jnp.float32(total_len) / lengths.astype(jnp.float32)
    token_weight = jnp.where(position < lengths[0], weight[0], jnp.float32(0.0))
    scaled_result = (grad_out[0].astype(jnp.float32) * token_weight[:, None]).astype(jnp.bfloat16)
    keys_all, values_all = (
        lax.all_gather(prompt_keys, "ctx", axis=0, tiled=True),
        lax.all_gather(prompt_value_rows, "ctx", axis=0, tiled=True),
    )
    query_pieces = queries[0].reshape(token_count, KEY_VALUE_HEADS, query_group_width * HEAD_SIZE)
    output_pieces = attention_output[0].reshape(
        token_count, KEY_VALUE_HEADS, query_group_width * HEAD_SIZE
    )
    gradient_pieces = scaled_result.reshape(
        token_count, KEY_VALUE_HEADS, query_group_width * HEAD_SIZE
    )
    own_term_pieces = own_log_sum_exp[0].reshape(token_count, KEY_VALUE_HEADS, query_group_width)
    query_list = []
    grad_list = []
    prob_list = []
    dscore_list = []
    query_parts = []
    for key_value_head in range(KEY_VALUE_HEADS):
        query_rows = query_pieces[:, key_value_head].reshape(
            token_count * query_group_width, HEAD_SIZE
        )
        grad_rows = gradient_pieces[:, key_value_head].reshape(
            token_count * query_group_width, HEAD_SIZE
        )
        output_rows = output_pieces[:, key_value_head].reshape(
            token_count * query_group_width, HEAD_SIZE
        )
        own_rows = own_term_pieces[:, key_value_head].reshape(token_count * query_group_width)
        keys_head = keys_all[:, key_value_head * HEAD_SIZE : (key_value_head + 1) * HEAD_SIZE]
        values_head = values_all[:, key_value_head * HEAD_SIZE : (key_value_head + 1) * HEAD_SIZE]
        prob_rows, dscores = prefix_terms(
            query_rows, grad_rows, output_rows, own_rows, keys_head, values_head, score_scale
        )
        query_term = jnp.dot(dscores, keys_head, preferred_element_type=jnp.float32) * score_scale
        query_parts.append(query_term.reshape(token_count, query_group_width * HEAD_SIZE))
        query_list.append(query_rows)
        grad_list.append(grad_rows)
        prob_list.append(prob_rows)
        dscore_list.append(dscores)
    query_grad = jnp.concatenate(query_parts, axis=1).astype(jnp.bfloat16)[None]
    key_terms = []
    value_terms = []
    for key_value_head in range(KEY_VALUE_HEADS):
        score_cols = dscore_list[key_value_head]
        prob_cols = prob_list[key_value_head]
        key_terms.append(contract_first(score_cols, query_list[key_value_head]) * score_scale)
        value_terms.append(contract_first(prob_cols, grad_list[key_value_head]))
    context_sum = lax.psum_scatter(
        jnp.concatenate(key_terms + value_terms, axis=1), "ctx", scatter_dimension=0, tiled=True
    )
    summed = lax.psum(context_sum, "resp")
    kv_width = prompt_keys.shape[1]
    key_grad = summed[:, :kv_width]
    value_grad = summed[:, kv_width:]
    final_grad = lax.psum_scatter(
        state_grad[0].astype(jnp.float32).astype(jnp.bfloat16),
        "resp",
        scatter_dimension=1,
        tiled=True,
    ).astype(jnp.float32)
    input_values = mamba_in.astype(jnp.float32)
    dy_values = mamba_grad.astype(jnp.float32)
    decay = jnp.exp(-step_size[:, None, :] * decay_rate[None, :, :])
    local_terms = output_map[:, :, None] * dy_values[:, None, :]

    def local_step(incoming, inputs):
        term_row, decay_row = inputs
        adjoint_row = term_row + incoming
        return (decay_row * adjoint_row, adjoint_row)

    passed, local_adjoint = lax.scan(
        local_step, jnp.zeros_like(final_grad), (local_terms, decay), reverse=True
    )
    step_total = jnp.sum(step_size, axis=0)
    span = jnp.exp(-step_total[None, :] * decay_rate)
    after = step_total[None, :] - jnp.cumsum(step_size, axis=0)
    reach = jnp.exp(-after[:, None, :] * decay_rate[None, :, :])
    before_span, before_passed = carried_in(
        (span, passed), "ctx", compose_maps, (jnp.ones_like(span), jnp.zeros_like(passed))
    )
    incoming = before_span * final_grad + before_passed
    adjoint = local_adjoint + reach * incoming[None]
    mamba_input_grad = step_size * jnp.sum(input_map[:, :, None] * adjoint, axis=1)
    db_part = jnp.sum(adjoint * (step_size * input_values)[:, None, :], axis=2)
    input_map_grad = lax.psum(db_part, "resp")
    return (query_grad, key_grad, value_grad, mamba_input_grad, input_map_grad)


def solution(mesh):
    placed = (
        P("resp", "ctx", None),
        P("resp", "ctx", None),
        P("resp", "ctx", None),
        P("resp", "ctx", None),
        P("ctx", None),
        P("ctx", None),
        P("resp"),
        P("resp"),
        P("ctx", "resp"),
        P("ctx", "resp"),
        P(None, "resp"),
        P("ctx", None),
        P("ctx", None),
        P("ctx", "resp"),
        P("resp", None, None),
    )
    return jax.shard_map(
        on_device,
        mesh=mesh,
        in_specs=placed,
        out_specs=(
            P("resp", "ctx", None),
            P("ctx", None),
            P("ctx", None),
            P("ctx", "resp"),
            P("ctx", None),
        ),
        check_vma=False,
    )
```

profile of v0, /device:TPU:6, one launch (start us, length us, event | category | flops | bytes accessed | tf_op | source)
XLA Modules:
  0.0 500.0 jit_solution(14156460369697748953)
XLA Ops:
  14.4 57.8 %all_gather.18 = bf16[512,512]{1,0:T(8,128)(2,1)} all-gather(bf16[16,512]{1,0:T(8,128)(2,1)S(1)} %copy-done.32), channel_id=1, replica_groups=mesh['ctx'=32,'resp'=16] {'ctx'}, dimensions={0}, use_global_device_ids=true | all-gather | bytes 540672 | tf_op jit(solution)/shard_map/all_gather | solution.py:84
  73.0 6.2 %slice_reduce_fusion.3 = (bf16[128,1024]{1,0:T(8,128)(2,1)S(1)}, bf16[128,1024]{1,0:T(8,128)(2,1)}, bf16[128,1024]{1,0:T(8,128)(2,1)}, bf16[128,1024]{1,0:T(8,128)(2,1)}) fusion(bf16[128,4,1024]{2,1,0:T(4,128)(2,1)S(1)} %reshape_squeeze.49), kind=kLoop, calls=%fused_computation.60 | loop fusion | bytes 2097152 | tf_op jit(solution)/shard_map/slice | solution.py:101
  82.1 1.7 reshape.224
  87.4 2.3 fusion.49
  90.9 51.5 %all_gather.19 = bf16[512,512]{1,0:T(8,128)(2,1)S(1)} all-gather(bf16[16,512]{1,0:T(8,128)(2,1)S(1)} %copy-done.33), channel_id=1, replica_groups=mesh['ctx'=32,'resp'=16] {'ctx'}, dimensions={0}, use_global_device_ids=true | all-gather | bytes 540672 | tf_op jit(solution)/shard_map/all_gather | solution.py:85
  142.4 1.5 multiply_reduce_fusion.3
  146.4 1.8 reshape_squeeze.55
  148.2 2.8 multiply_reduce_fusion.2
  151.8 1.8 reshape_squeeze.57
  153.6 1.9 reshape.226
  155.5 1.8 reshape_squeeze.58
  157.3 2.7 multiply_reduce_fusion.1
  160.8 1.8 reshape_squeeze.60
  162.6 2.4 copy_convert_fusion
  165.0 1.9 reshape.227
  166.9 1.8 reshape_squeeze.61
  168.6 2.9 multiply_reduce_fusion
  173.0 1.8 reshape_squeeze.63
  174.7 1.9 reshape.228
  176.7 2.1 exponential_reduce_fusion.2
  178.8 1.4 multiply_reduce_fusion.8
  190.2 1.3 convolution_dynamic-update-slice_fusion.2
  194.0 3.0 copy.68
  197.8 1.4 fusion.5
  200.0 1.5 fusion.6
  201.6 1.4 fusion.7
  203.2 1.4 fusion.8
  205.8 5.8 %while.31 = (s32[]{:T(128)}, f32[16,512]{1,0:T(8,128)S(1)}, f32[16,512]{1,0:T(8,128)S(1)}, s32[]{:T(128)}, f32[32,16,512]{2,1,0:T(8,128)}, /*index=5*/f32[32,16,...) while((s32[]{:T(128)}, f32[16,512]{1,0:T(8,128)S(1)}, f32[16,512]{1,0:T(8,128)S(1)}, ...), condition=%wide.region_19.20_spmd, body=%wide.region_18.19_spmd.sunk | while | flops 24582 | bytes 196759 | solution.py:26
  212.4 106.8 %reduce-scatter.7.cloned.1.call-done = f32[16,1024]{1,0:T(8,128)} async-done(((f32[512,1024]{1,0:T(8,128)}), f32[16,1024]{1,0:T(8,128)}) %reduce-scatter.7.cloned.1.call-update) | async-done | bytes 65552
  319.2 1.9 copy.69
  321.9 43.5 %psum.15 = f32[16,16]{1,0:T(8,128)} all-reduce(f32[16,16]{1,0:T(8,128)S(1)} %get-tuple-element.231), channel_id=1, replica_groups=mesh['ctx'=32,'resp'=16] {'resp'}, use_global_device_ids=true, to_apply=%region_23.24 | all-reduce | flops 256 | bytes 2048 | tf_op jit(solution)/shard_map/psum | solution.py:167
  365.5 124.5 %all-reduce.2.cloned.1.call-done = f32[16,1024]{0,1:T(8,128)} async-done(((f32[16,1024]{0,1:T(8,128)}), f32[16,1024]{0,1:T(8,128)}) %all-reduce.2.cloned.1.call-update) | async-done | bytes 65552 | tf_op jit(solution)/shard_map/psum | solution.py:133
  (193 shorter events, 44.4 us)
Async XLA Ops:
  8.0 5.1 %copy-start.28 = (f32[16,512]{1,0:T(8,128)S(1)}, f32[16,512]{1,0:T(8,128)}, u32[]{:S(2)}) copy-start(f32[16,512]{1,0:T(8,128)} %param.29) | copy-start | bytes 98308
  8.0 6.4 %copy-start.32 = (bf16[16,512]{1,0:T(8,128)(2,1)S(1)}, bf16[16,512]{1,0:T(8,128)(2,1)}, u32[]{:S(2)}) copy-start(bf16[16,512]{1,0:T(8,128)(2,1)} %param.23) | copy-start | bytes 49156
  8.0 64.2 %copy-start.25 = (bf16[1,128,4096]{2,1,0:T(8,128)(2,1)S(1)}, bf16[1,128,4096]{2,1,0:T(8,128)(2,1)}, u32[]{:S(2)}) copy-start(bf16[1,128,4096]{2,1,0:T(8,128)(2,1)} %param.19) | copy-start | bytes 3145732
  8.0 197.8 %all-gather.7.cloned.1.call-start = ((), (), s32[]{:S(2)}) async-start(), calls=%async_computation.5 | async-start | bytes 1081344 | tf_op jit(solution)/shard_map/all_gather | solution.py:17
  9.7 62.5 %copy-start.30 = (f32[512]{0:T(512)}, f32[512]{0:T(512)S(1)}, u32[]{:S(2)}) copy-start(f32[512]{0:T(512)S(1)} %get-tuple-element.267) | copy-start | bytes 6148
  12.4 2.0 copy-start.22
  13.0 192.8 %all-gather.5.cloned.1.call-start = ((), (), s32[]{:S(2)}) async-start(), calls=%async_computation.4 | async-start | bytes 1081344 | tf_op jit(solution)/shard_map/all_gather | solution.py:17
  13.8 197.9 %reduce-scatter.5.cloned.1.call-start = ((), (), s32[]{:S(2)}) async-start(), calls=%async_computation.3 | async-start | bytes 278528 | tf_op jit(solution)/shard_map/reduce_scatter | solution.py:137
  14.3 304.9 %reduce-scatter.7.cloned.1.call-start = ((), (), s32[]{:S(2)}) async-start(), calls=%async_computation.6 | async-start | bytes 2162688
  73.0 7.0 %copy-start.34 = (f32[1,128,32]{1,2,0:T(8,128)S(1)}, f32[1,128,32]{1,2,0:T(8,128)}, u32[]{:S(2)}) copy-start(f32[1,128,32]{1,2,0:T(8,128)} %param.22) | copy-start | bytes 49156
  73.0 9.1 %copy-start.24 = (bf16[1,128,4096]{2,1,0:T(8,128)(2,1)S(1)}, bf16[1,128,4096]{2,1,0:T(8,128)(2,1)}, u32[]{:S(2)}) copy-start(bf16[1,128,4096]{2,1,0:T(8,128)(2,1)} %param.21) | copy-start | bytes 3145732
  89.8 52.6 %copy-start.13 = (bf16[1024,128]{1,0:T(8,128)(2,1)S(1)}, bf16[1024,128]{1,0:T(8,128)(2,1)}, u32[]{:S(2)}) copy-start(bf16[1024,128]{1,0:T(8,128)(2,1)} %reshape_squeeze.50) | copy-start | bytes 786436
  142.4 2.1 copy-start.18
  173.0 5.8 %copy-start.35 = (f32[1024]{0:T(1024)S(1)}, f32[1024]{0:T(1024)}, u32[]{:S(2)}) copy-start(f32[1024]{0:T(1024)} %reshape_squeeze.56) | copy-start | bytes 12292
  176.7 3.5 copy-start
  176.7 3.5 copy-start.9
  176.7 3.5 copy-start.19
  178.8 3.0 copy-start.15
  180.2 2.8 copy-start.1
  181.8 1.6 copy-start.10
  181.8 1.6 copy-start.20
  183.4 1.8 copy-start.16
  183.6 2.8 copy-start.2
  187.8 2.4 copy-start.7
  197.0 3.0 copy-start.4
  197.0 4.6 copy-start.6
  197.0 292.9 %all-reduce.2.cloned.1.call-start = ((), (), s32[]{:S(2)}) async-start(), calls=%async_computation.2 | async-start | bytes 1048576 | tf_op jit(solution)/shard_map/psum | solution.py:133
  200.0 3.2 copy-start.8
  201.6 3.1 copy-start.31
  201.6 3.1 copy-start.27
  204.8 116.3 %copy-start.23 = (f32[16,16,512]{2,1,0:T(8,128)S(1)}, f32[16,16,512]{2,1,0:T(8,128)}, u32[]{:S(2)}) copy-start(f32[16,16,512]{2,1,0:T(8,128)} %copy-done.22) | copy-start | bytes 1572868
  204.8 116.3 %copy-start.38 = (f32[16,16]{1,0:T(8,128)S(1)}, f32[16,16]{1,0:T(8,128)}, u32[]{:S(2)}) copy-start(f32[16,16]{1,0:T(8,128)} %param.30) | copy-start | bytes 3076
  (12 other events, 14.2 us)
Sparse Core Ops, SparseCore 0:
  13.1 75.2 all-gather.6
  92.1 65.9 all-gather.4
Sparse Core Ops, SparseCore 1:
  17.0 94.3 reduce-scatter.4
  197.1 122.1 reduce-scatter.6
  322.2 167.7 all-reduce.1
where the time goes:
time: 503 us; the launch traced here: 500 us
  waiting for transfers between devices  232 us (46%)
  blocking collectives  153 us (30%)
  local copies, waits for them, and re-layouts  46.4 us (9%)
  matrix products  27.6 us (5%)
  other arithmetic  22.5 us (4%)
  between operations  17.6 us (3%)
    psum x1, waiting for transfers between devices, on_device(): summed = lax.psum(context_sum, 'resp')  124 us
    unnamed x6, waiting for transfers between devices  107 us
    all_gather x1, blocking collectives, on_device(): lax.all_gather(prompt_keys, 'ctx', axis=0, tiled=True)  57.8 us
    all_gather x1, blocking collectives, on_device(): lax.all_gather(prompt_value_rows, 'ctx', axis=0, tiled=True)  51.5 us
    psum x1, blocking collectives, on_device(): input_map_grad = lax.psum(db_part, 'resp')  43.5 us
    dot_general x8, matrix products, contract_last(): lax.dot_general(left, right, (((1,), (1,)), ((), ())), preferred_element_...  12.2 us
    unnamed x86, local copies, waits for them, and re-layouts  11.3 us
  transfers between devices with their start and end apart: 5, of which 2 were waited for; matrix products, arithmetic and copies ran while one was open for 17% of the time, Pallas kernels for 0%

commit v1 on v0

v1 whole, which is shorter than its diff:
```python
import functools
import math

import jax
import jax.numpy as jnp
from jax import lax
from jax.experimental import pallas as pl
from jax.experimental.pallas import tpu as pltpu
from jax.sharding import PartitionSpec as P

X, Y, Z, ZH, ZL, CORES, RESP = 4, 4, 16, 4, 4, 2, 16
GROUP = ZH * CORES
HEADS, KV_HEADS, SIZE = 32, 4, 128
PER_KV = HEADS // KV_HEADS
TOKENS = 128
KEYS = 512
BLOCK = 16
STATE = 16
LANES = 128
CHANNELS = 512
SCALE = 1.0 / math.sqrt(SIZE)
LOG2E = math.log2(math.e)
F32 = jnp.float32
BF16 = jnp.bfloat16
MESH = pl.DeviceIdType.MESH
NT = (((1,), (1,)), ((), ()))
VMEM = pl.BlockSpec(memory_space=pltpu.VMEM)


def place():
    ctx = lax.axis_index("ctx")
    resp = lax.axis_index("resp")
    x = lax.div(ctx, GROUP)
    q = lax.rem(ctx, GROUP)
    zh = lax.div(q, CORES)
    c = lax.rem(q, CORES)
    zl = lax.div(resp, Y)
    y = lax.rem(resp, Y)
    return ctx, resp, x, q, zh, c, zl, y


def step(value, offset, count):
    return lax.rem(value + offset + count, count)


LINE, AY, AX, CORE, STATES, TILES, MAPS, BACKS, SUMS = 0, 1, 2, 3, 5, 6, 7, 8, 9
BX, BY, HALVES = 10, 16, 22
FIRST, SECOND, LINES, PIECES = 26, 30, 34, 36
SEMS = 38


def kernel(
    advantages, lengths, queries_h, outputs_h, grads_h, own_h, keys_h, values_h, mamba_in_h, step_h, rate_h,
    input_map_h, output_map_h, mamba_grad_h, state_h,
    query_grad, key_grad, value_grad, mamba_out, map_out,
    queries, outputs, grads, own, keys, values, mamba_in, step_size, decay_rate, input_map, output_map, mamba_grad,
    state_own, blocks, kv, own_t, inners, square, square_in, decays, tiles_out, tiles_in, state_in,
    group_out, group_in, back_out, back_in, db_out, db_in,
    partial, core_in, pairs, first_in, firsts, second_in, lines, line_in, piece, pieces, query_out,
    load_sem, store_sem, send_sem, recv_sem,
):
    ctx, resp, x, q, zh, c, zl, y = place()
    other = 1 - c
    z = zh * ZL + zl

    xs = [(step(x, d, X) * GROUP + q, resp) for d in range(1, X)]
    ys = [(ctx, zl * Y + step(y, d, Y)) for d in range(1, Y)]
    zs = [(x * GROUP + step(zh, d, ZH) * CORES + c, resp) for d in range(1, ZH)]
    partner = (x * GROUP + zh * CORES + other, resp)

    def group(d):
        return (x * GROUP + step(q, d, GROUP), resp)

    def resps(d):
        return (ctx, step(resp, d, RESP))

    def each(count, act):
        def one(d, carry):
            act(d)
            return carry

        lax.fori_loop(1, count, one, 0)

    mine = pl.multiple_of(resp * CHANNELS + zh * LANES, LANES)
    loads = [
        (keys_h, keys), (values_h, values), (step_h, step_size), (rate_h, decay_rate), (output_map_h, output_map),
        (mamba_grad_h, mamba_grad), (grads_h, grads), (outputs_h, outputs), (own_h, own), (queries_h, queries),
        (mamba_in_h, mamba_in), (input_map_h, input_map), (state_h.at[0, :, pl.ds(mine, LANES)], state_own),
    ]
    loads = [pltpu.make_async_copy(src, dst, load_sem.at[i]) for i, (src, dst) in enumerate(loads)]
    for load in loads:
        load.start()
    wide = PER_KV * SIZE

    def store(g):
        cols = pl.ds(pl.multiple_of(g * wide, wide), wide)
        return pltpu.make_async_copy(query_out.at[0, :, cols], query_grad.at[0, :, cols], store_sem.at[g])

    barrier = pltpu.get_barrier_semaphore()

    def greet(target):
        pl.semaphore_signal(barrier, inc=1, device_id=target, device_id_type=MESH)

    for target in xs:
        greet(target)
    each(GROUP, lambda d: greet(group(d)))
    each(RESP, lambda d: greet(resps(d)))
    for j in range(1, ZL):
        each(ZH, lambda d: greet((x * GROUP + step(zh, d, ZH) * CORES + c, step(zl, j, ZL) * Y + y)))
    partners = 3 + 7 + 15 + 9

    def send(src, dst, target, sem, recv=None):
        pltpu.make_async_remote_copy(
            src_ref=src, dst_ref=dst, send_sem=send_sem.at[sem], recv_sem=recv_sem.at[sem if recv is None else recv],
            device_id=target, device_id_type=MESH,
        ).start()

    def arrived(ref, sem):
        pltpu.make_async_remote_copy(
            src_ref=ref, dst_ref=ref, send_sem=send_sem.at[sem], recv_sem=recv_sem.at[sem],
            device_id=partner, device_id_type=MESH,
        ).wait_recv()

    def left(ref, sem):
        pltpu.make_async_remote_copy(
            src_ref=ref, dst_ref=ref, send_sem=send_sem.at[sem], recv_sem=recv_sem.at[sem],
            device_id=partner, device_id_type=MESH,
        ).wait_send()

    loads[0].wait()
    loads[1].wait()
    for ch in range(2):
        for kind in range(2):
            for gl in range(2):
                g = ch * 2 + gl
                blocks[ch, kind * 2 + gl] = (keys, values)[kind][:, g * LANES:(g + 1) * LANES]
    kv[:, y, c, x, zh] = blocks[:, y]
    pl.semaphore_wait(barrier, partners)
    for d in range(1, ZH):
        send(blocks.at[:, y], kv.at[:, y, c, x, zh], zs[d - 1], LINE)

    for i in range(2, 6):
        loads[i].wait()
    square[...] = jnp.zeros_like(square)
    square[0:16, 0:16] = output_map[...]
    out_t = square[...].T
    rate = decay_rate[...]
    steps = step_size[...]
    dy = mamba_grad[...].astype(F32)
    carry = jnp.zeros((STATE, CHANNELS), F32)
    for t in range(BLOCK - 1, -1, -1):
        decay = jnp.exp(-steps[t:t + 1] * rate)
        decays[t] = decay
        carry = decay * (out_t[0:STATE, t:t + 1] * dy[t:t + 1] + carry)
    span = jnp.exp(-jnp.sum(steps, axis=0, keepdims=True) * rate)
    for k in range(GROUP):
        kt, nh = k // 2, k % 2
        tiles_out[k, 0] = carry[nh * 8:nh * 8 + 8, kt * LANES:(kt + 1) * LANES]
        tiles_out[k, 1] = span[nh * 8:nh * 8 + 8, kt * LANES:(kt + 1) * LANES]
    each(GROUP, lambda d: send(tiles_out.at[step(q, d, GROUP)], tiles_in.at[q], group(d), TILES))
    tiles_in[q] = tiles_out[q]

    arrived(kv.at[:, y, c, x, 0:3], LINE)
    for d in range(1, 4):
        here = kv.at[:, y, c, x, 0:2]
        send(here, here, ys[d - 1], AY)
        here = kv.at[:, y, c, x, 2:4]
        send(here, here, xs[d - 1], AX)

    length = lengths[0]
    weight = advantages[0] * F32(TOKENS * lax.axis_size("ctx")) / length.astype(F32)
    position = ctx * TOKENS + lax.broadcasted_iota(jnp.int32, (TOKENS, 1), 0)
    token_weight = jnp.where(position < length, weight, F32(0.0))
    ones = jnp.ones((8, SIZE), BF16)

    def prepare(quad, carry):
        for i in range(4):
            h = quad * 4 + i
            cols = pl.ds(pl.multiple_of(h * SIZE, SIZE), SIZE)
            scaled = (grads[0, :, cols].astype(F32) * token_weight).astype(BF16)
            grads[0, :, cols] = scaled
            product = scaled.astype(F32) * outputs[0, :, cols].astype(F32)
            high = product.astype(BF16)
            low = (product - high.astype(F32)).astype(BF16)
            inners[h] = (
                lax.dot_general(ones, high, NT, preferred_element_type=F32)
                + lax.dot_general(ones, low, NT, preferred_element_type=F32)
            )
        return carry

    for i in range(6, 9):
        loads[i].wait()
    own_t[...] = own[0] * LOG2E
    lax.fori_loop(0, 4, prepare, 0)

    arrived(kv.at[:, 0:3, c, x, 0:2], AY)
    arrived(kv.at[:, y, c, 0:3, 2:4], AX)
    for ch in range(2):
        by_x = kv.at[ch, :, c, x, 0:2]
        by_y = kv.at[ch, y, c, :, 2:4]
        for d in range(1, 4):
            send(by_x, by_x, xs[d - 1], BX + 3 * ch, BX + 3 * ch + d - 1)
            send(by_y, by_y, ys[d - 1], BY + 3 * ch, BY + 3 * ch + d - 1)
        send(by_x, by_x, partner, CORE + ch)
        send(by_y, by_y, partner, CORE + ch)

    def send_state(d):
        start = pl.multiple_of(step(resp, d, RESP) * CHANNELS + zh * LANES, LANES)
        send(state_h.at[0, :, pl.ds(start, LANES)], state_in.at[d - 1], resps(d), STATES)

    each(RESP, send_state)

    arrived(tiles_in.at[0:7], TILES)
    span_all = jnp.ones((8, LANES), F32)
    carry_all = jnp.zeros((8, LANES), F32)
    for k in range(GROUP - 1, -1, -1):
        carry_all = tiles_in[k, 1] * carry_all + tiles_in[k, 0]
        span_all = span_all * tiles_in[k, 1]
    group_out[0] = carry_all
    group_out[1] = span_all
    for d in range(1, X):
        send(group_out, group_in.at[x], xs[d - 1], MAPS)
    group_in[x] = group_out[...]

    def pass_on(ch):
        for d in range(1, 4):
            here = kv.at[ch, :, c, step(x, -d, X), 0:2]
            arrived(here, BX + 3 * ch + d - 1)
            send(here, here, partner, CORE + ch)
            here = kv.at[ch, step(y, -d, Y), c, :, 2:4]
            arrived(here, BY + 3 * ch + d - 1)
            send(here, here, partner, CORE + ch)

    def carry_back():
        for i in range(10, 13):
            loads[i].wait()
        arrived(state_in.at[0:15], STATES)
        arrived(group_in.at[0:3], MAPS)
        final = state_own[...].astype(F32) + jnp.sum(state_in[...].astype(F32), axis=0)
        incoming = jnp.where(c == 0, final[0:8], final[8:16])
        for k in range(X - 1, 0, -1):
            passed = group_in[k, 1] * incoming + group_in[k, 0]
            incoming = jnp.where(x < k, passed, incoming)
        for k in range(GROUP - 1, -1, -1):
            back_out[k] = incoming
            incoming = tiles_in[k, 1] * incoming + tiles_in[k, 0]
        each(GROUP, lambda d: send(back_out.at[step(q, d, GROUP)], back_in.at[q], group(d), BACKS))
        back_in[q] = back_out[q]

    def rows(ref, pair):
        heads = (2 * pair, 2 * pair + 1)
        return jnp.concatenate([ref[0, :, h * SIZE:(h + 1) * SIZE] for h in heads], axis=0)

    def keys_of(g):
        return kv[g // 2, g % 2].reshape(KEYS, SIZE)

    def begin(pair):
        g = pair // 4
        values_g = kv[g // 2, 2 + g % 2].reshape(KEYS, SIZE)
        scores = lax.dot_general(keys_of(g), rows(queries, pair), NT, preferred_element_type=F32) * (SCALE * LOG2E)
        dprobs = lax.dot_general(values_g, rows(grads, pair), NT, preferred_element_type=F32)
        return scores, dprobs

    def end(pair, begun, transposed, sums):
        scores, dprobs = begun
        h = 2 * pair
        inner = jnp.concatenate([inners[h, 0:1], inners[h + 1, 0:1]], axis=1)
        own2 = jnp.concatenate([own_t[h:h + 1], own_t[h + 1:h + 2]], axis=1)
        top = jnp.maximum(jnp.max(scores, axis=0, keepdims=True), own2)
        powers = jnp.exp2(scores - top)
        total = jnp.sum(powers, axis=0, keepdims=True) + jnp.exp2(own2 - top)
        probs = powers * (1.0 / total)
        dscores = (probs * (dprobs - inner)).astype(BF16)
        query_t = jnp.dot(transposed, dscores, preferred_element_type=F32) * SCALE
        for i in range(2):
            part = query_t[:, i * SIZE:(i + 1) * SIZE].T.astype(BF16)
            query_out[0, :, (h + i) * SIZE:(h + i + 1) * SIZE] = part
        return (
            sums[0] + jnp.dot(dscores, rows(queries, pair), preferred_element_type=F32),
            sums[1] + jnp.dot(probs.astype(BF16), rows(grads, pair), preferred_element_type=F32),
        )

    def ship(g, sums):
        ch, gl = g // 2, g % 2
        for kind in range(2):
            partial[ch, kind, gl] = sums[kind].astype(BF16).reshape(partial.shape[3:])
        send(partial.at[ch, :, gl, other], core_in.at[ch, :, gl], partner, HALVES + g)
        store(g).start()

    def join(g):
        ch, gl = g // 2, g % 2
        arrived(core_in.at[ch, :, gl], HALVES + g)
        for kind in range(2):
            pairs[ch, kind * 2 + gl] = (
                partial[ch, kind, gl, c].astype(F32) + core_in[ch, kind, gl].astype(F32)
            ).astype(BF16)

    def first_hop(ch):
        for d in range(1, 4):
            send(pairs.at[ch, :, step(x, d, X), 0:2], first_in.at[ch, 0, d - 1], xs[d - 1], FIRST + 2 * ch)
            send(pairs.at[ch, step(y, d, Y), :, 2:4], first_in.at[ch, 1, d - 1], ys[d - 1], FIRST + 2 * ch + 1)

    def second_hop(ch):
        for axis in range(2):
            arrived(first_in.at[ch, axis], FIRST + 2 * ch + axis)
            held = pairs[ch, :, x, 0:2] if axis == 0 else pairs[ch, y, :, 2:4]
            total = held.astype(F32)
            for d in range(3):
                total = total + first_in[ch, axis, d].astype(F32)
            firsts[ch, axis] = total.astype(BF16)
            for d in range(1, 4):
                to = step(y, d, Y) if axis == 0 else step(x, d, X)
                target = (ys if axis == 0 else xs)[d - 1]
                send(firsts.at[ch, axis, to], second_in.at[ch, axis, d - 1], target, SECOND + 2 * ch + axis)

    def to_lines(ch):
        for axis in range(2):
            arrived(second_in.at[ch, axis], SECOND + 2 * ch + axis)
            total = firsts[ch, axis, y if axis == 0 else x].astype(F32)
            for d in range(3):
                total = total + second_in[ch, axis, d].astype(F32)
            lines[ch, 2 * axis:2 * axis + 2] = total.astype(BF16)
        for i in range(1, ZH):
            to = step(zh, i, ZH)
            send(lines.at[ch, to], line_in.at[z], (x * GROUP + to * CORES + c, (1 + ch) * Y + y), LINES + ch)

        @pl.when(zl != 1 + ch)
        def _():
            send(lines.at[ch, zh], line_in.at[z], (ctx, (1 + ch) * Y + y), LINES + ch)

    def sum_line(ch):
        @pl.when(zl == 1 + ch)
        def _():
            line_in[z] = lines[ch, zh]
            arrived(line_in.at[0:15], LINES + ch)
            summed = jnp.sum(line_in[...].astype(F32), axis=0)
            piece[...] = summed
            each(RESP, lambda d: send(piece, pieces.at[ch * Y + y], resps(d), PIECES + ch))
            pieces[ch * Y + y] = summed

    loads[9].wait()
    pass_on(0)
    lax.fori_loop(4, 8, prepare, 0)
    arrived(kv.at[0, :, other], CORE)
    begun = begin(0)
    for pair in range(HEADS // 2):
        g = pair // 4
        if pair % 4 == 0:
            transposed = keys_of(g).T
            sums = (jnp.zeros((KEYS, SIZE), F32),) * 2
        if pair == 3:
            pass_on(1)
        if pair == 7:
            arrived(kv.at[1, :, other], CORE + 1)
        ahead = begin(pair + 1) if pair + 1 < HEADS // 2 else None
        sums = end(pair, begun, transposed, sums)
        begun = ahead
        if pair % 4 == 3:
            ship(g, sums)
            if g == 1:
                join(0)
                carry_back()
            if g == 2:
                join(1)
                first_hop(0)
    join(2)
    second_hop(0)
    join(3)
    first_hop(1)
    to_lines(0)

    arrived(back_in.at[0:7], BACKS)
    square_in[...] = jnp.zeros_like(square_in)
    square_in[0:16, 0:16] = input_map[...]
    in_t = square_in[...].T
    taken = steps * mamba_in[...].astype(F32)
    carry = jnp.concatenate(
        [jnp.concatenate([back_in[kt * 2 + nh] for kt in range(4)], axis=1) for nh in range(2)], axis=0
    )
    lane = lax.broadcasted_iota(jnp.int32, (STATE, LANES), 1)
    db = jnp.zeros((STATE, LANES), F32)
    for t in range(BLOCK - 1, -1, -1):
        adjoint = out_t[0:STATE, t:t + 1] * dy[t:t + 1] + carry
        total = jnp.sum(in_t[0:STATE, t:t + 1] * adjoint, axis=0, keepdims=True)
        mamba_out[t:t + 1, :] = steps[t:t + 1] * total
        term = adjoint * taken[t:t + 1]
        term = (term[:, 0:128] + term[:, 128:256]) + (term[:, 256:384] + term[:, 384:512])
        db = jnp.where(lane == t, jnp.sum(term, axis=1, keepdims=True), db)
        carry = decays[t] * adjoint
    db_out[...] = db

    second_hop(1)
    each(RESP, lambda d: send(db_out, db_in.at[d - 1], resps(d), SUMS))
    to_lines(1)
    sum_line(0)
    arrived(db_in.at[0:15], SUMS)
    square[0:STATE, :] = db_out[...] + jnp.sum(db_in[...], axis=0)
    map_out[...] = square[...].T[0:16, 0:16]
    sum_line(1)

    left(blocks.at[:, 0:3], LINE)
    left(tiles_out.at[0:7], TILES)
    left(kv.at[:, 0:3, c, x, 0:2], AY)
    left(kv.at[:, y, c, 0:3, 2:4], AX)
    left(state_in.at[0:15], STATES)
    for ch in range(2):
        left(kv.at[ch, :, c, 0:3, 0:2], BX + 3 * ch)
        left(kv.at[ch, 0:3, c, :, 2:4], BY + 3 * ch)
        left(kv.at[ch, :, c], CORE + ch)
    left(group_in.at[0:3], MAPS)
    left(back_out.at[0:7], BACKS)
    for g in range(KV_HEADS):
        left(core_in.at[g // 2, :, g % 2], HALVES + g)
    for ch in range(2):
        for axis in range(2):
            left(first_in.at[ch, axis], FIRST + 2 * ch + axis)
            left(second_in.at[ch, axis], SECOND + 2 * ch + axis)
    left(db_in.at[0:15], SUMS)
    for ch in range(2):

        @pl.when(zl == 1 + ch)
        def _():
            left(line_in.at[0:3], LINES + ch)
            left(db_in.at[0:15], PIECES + ch)

        @pl.when(zl != 1 + ch)
        def _():
            left(line_in.at[0:4], LINES + ch)

    for g in range(KV_HEADS):
        store(g).wait()

    for ch in range(2):

        @pl.when(zl == 1 + ch)
        def _():
            arrived(pieces.at[0:3], PIECES + ch)

        @pl.when(zl != 1 + ch)
        def _():
            arrived(pieces.at[0:4], PIECES + ch)

        for gl in range(2):
            cols = slice((ch * 2 + gl) * LANES, (ch * 2 + gl + 1) * LANES)
            key_grad[:, cols] = pieces[ch * Y + gl] * SCALE
            value_grad[:, cols] = pieces[ch * Y + 2 + gl]


def finish_kernel(*refs):
    given, results, held = refs[0:5], refs[5:10], refs[10:15]
    sem_in, sem_out = refs[15], refs[16]
    part = (given[0].at[0], held[0].at[0], results[0].at[0])
    moves = [(given[i], held[i], results[i]) for i in range(1, 5)]
    for i in range(8):
        rows = slice(i * BLOCK, (i + 1) * BLOCK)
        moves.append(tuple(ref.at[rows] for ref in part))
    copies_in = [pltpu.make_async_copy(src, mid, sem_in.at[i]) for i, (src, mid, _) in enumerate(moves)]
    copies_out = [pltpu.make_async_copy(mid, dst, sem_out.at[i]) for i, (_, mid, dst) in enumerate(moves)]
    for copy in copies_in:
        copy.start()
    for first, then in zip(copies_in, copies_out):
        first.wait()
        then.start()
    for copy in copies_out:
        copy.wait()


def on_device(
    queries, attention_output, grad_out, own_log_sum_exp, prompt_keys, prompt_value_rows, advantages, lengths,
    mamba_in, step_size, decay_rate, input_map, output_map, mamba_grad, state_grad,
):
    smem = pl.BlockSpec(memory_space=pltpu.SMEM)
    anywhere = pl.BlockSpec(memory_space=pl.ANY)
    tile = (ZH, BLOCK, LANES)
    half = (2, BLOCK, LANES)
    wide = (1, TOKENS, HEADS * SIZE)
    block_grad = jax.ShapeDtypeStruct((BLOCK, KV_HEADS * SIZE), F32)
    results = (
        jax.ShapeDtypeStruct(wide, BF16),
        block_grad,
        block_grad,
        jax.ShapeDtypeStruct((BLOCK, CHANNELS), F32),
        jax.ShapeDtypeStruct((BLOCK, STATE), F32),
    )
    computed = pl.pallas_call(
        kernel,
        out_shape=results,
        in_specs=[smem] * 2 + [anywhere] * 13,
        out_specs=(anywhere,) + (VMEM,) * 4,
        scratch_shapes=[
            pltpu.VMEM(wide, BF16),
            pltpu.VMEM(wide, BF16),
            pltpu.VMEM(wide, BF16),
            pltpu.VMEM((1, HEADS, TOKENS), F32),
            pltpu.VMEM((BLOCK, KV_HEADS * SIZE), BF16),
            pltpu.VMEM((BLOCK, KV_HEADS * SIZE), BF16),
            pltpu.VMEM((BLOCK, CHANNELS), BF16),
            pltpu.VMEM((BLOCK, CHANNELS), F32),
            pltpu.VMEM((STATE, CHANNELS), F32),
            pltpu.VMEM((BLOCK, STATE), F32),
            pltpu.VMEM((BLOCK, STATE), F32),
            pltpu.VMEM((BLOCK, CHANNELS), BF16),
            pltpu.VMEM((STATE, LANES), BF16),
            pltpu.VMEM((2, 4, BLOCK, LANES), BF16),
            pltpu.VMEM((2, 4, CORES, X) + tile, BF16),
            pltpu.VMEM((HEADS, TOKENS), F32),
            pltpu.VMEM((HEADS, 8, TOKENS), F32),
            pltpu.VMEM((LANES, LANES), F32),
            pltpu.VMEM((LANES, LANES), F32),
            pltpu.VMEM((BLOCK, STATE, CHANNELS), F32),
            pltpu.VMEM((GROUP, 2, 8, LANES), F32),
            pltpu.VMEM((GROUP, 2, 8, LANES), F32),
            pltpu.VMEM((RESP - 1, STATE, LANES), BF16),
            pltpu.VMEM((2, 8, LANES), F32),
            pltpu.VMEM((X, 2, 8, LANES), F32),
            pltpu.VMEM((GROUP, 8, LANES), F32),
            pltpu.VMEM((GROUP, 8, LANES), F32),
            pltpu.VMEM((STATE, LANES), F32),
            pltpu.VMEM((RESP - 1, STATE, LANES), F32),
            pltpu.VMEM((2, 2, 2, CORES, X) + tile, BF16),
            pltpu.VMEM((2, 2, 2, X) + tile, BF16),
            pltpu.VMEM((2, 4, X) + tile, BF16),
            pltpu.VMEM((2, 2, 3, 4) + half, BF16),
            pltpu.VMEM((2, 2, 4) + half, BF16),
            pltpu.VMEM((2, 2, 3) + half, BF16),
            pltpu.VMEM((2,) + tile, BF16),
            pltpu.VMEM((Z, BLOCK, LANES), BF16),
            pltpu.VMEM((BLOCK, LANES), F32),
            pltpu.VMEM((2 * Y, BLOCK, LANES), F32),
            pltpu.VMEM(wide, BF16),
            pltpu.SemaphoreType.DMA((13,)),
            pltpu.SemaphoreType.DMA((KV_HEADS,)),
            pltpu.SemaphoreType.DMA((SEMS,)),
            pltpu.SemaphoreType.DMA((SEMS,)),
        ],
        compiler_params=pltpu.CompilerParams(
            collective_id=0, has_side_effects=True, vmem_limit_bytes=56 * 2**20
        ),
        name="whole",
    )(
        advantages, lengths, queries, attention_output, grad_out, jnp.swapaxes(own_log_sum_exp, 1, 2), prompt_keys,
        prompt_value_rows, mamba_in, step_size, decay_rate, input_map, output_map, mamba_grad, state_grad,
    )
    return pl.pallas_call(
        finish_kernel,
        out_shape=results,
        in_specs=[anywhere] * 5,
        out_specs=(anywhere,) * 5,
        scratch_shapes=[pltpu.VMEM(r.shape, r.dtype) for r in results]
        + [pltpu.SemaphoreType.DMA((12,)), pltpu.SemaphoreType.DMA((12,))],
        compiler_params=pltpu.CompilerParams(vmem_limit_bytes=60 * 2**20),
        name="finish",
    )(*computed)


def solution(mesh):
    placed = (
        P("resp", "ctx", None),
        P("resp", "ctx", None),
        P("resp", "ctx", None),
        P("resp", "ctx", None),
        P("ctx", None),
        P("ctx", None),
        P("resp"),
        P("resp"),
        P("ctx", "resp"),
        P("ctx", "resp"),
        P(None, "resp"),
        P("ctx", None),
        P("ctx", None),
        P("ctx", "resp"),
        P("resp", None, None),
    )
    return jax.shard_map(
        on_device,
        mesh=mesh,
        in_specs=placed,
        out_specs=(
            P("resp", "ctx", None),
            P("ctx", None),
            P("ctx", None),
            P("ctx", "resp"),
            P("ctx", None),
        ),
        check_vma=False,
    )
```

time: 503 us -> 70 us (0.14)
  waiting for transfers between devices: 232 us -> 0 us
  blocking collectives: 153 us -> 0 us
  Pallas kernels: 0 us -> 67.1 us
  local copies, waits for them, and re-layouts: 46.4 us -> 0 us
  matrix products: 27.6 us -> 0 us
  other arithmetic: 22.5 us -> 0 us
  between operations: 17.6 us -> 1.94 us
    psum x1 -> x0, waiting for transfers between devices: 124 us -> none  [on_device(): summed = lax.psum(context_sum, 'resp')]
    all_gather x2 -> x0, blocking collectives: 109 us -> none  [the longest x1 57.8 us: on_device(): lax.all_gather(prompt_keys, 'ctx', axis=0, tiled=True)]
    unnamed x6 -> x0, waiting for transfers between devices: 107 us -> none
    pallas_call x0 -> x2, Pallas kernels: none -> 67.1 us  [the longest x1 64.9 us: on_device(): pl.pallas_call(kernel, out_shape=results, in_specs=[smem] * 2 + [anywhere...]
    psum x1 -> x0, blocking collectives: 43.5 us -> none  [on_device(): input_map_grad = lax.psum(db_part, 'resp')]
    dot_general x20 -> x0, matrix products: 27.6 us -> none  [the longest x8 12.2 us: contract_last(): lax.dot_general(left, right, (((1,), (1,)), ((), ())), preferred_element_...]
    another operation x15 -> x0, local copies, waits for them, and re-layouts: 15.3 us -> none  [the longest x4 6.17 us: on_device(): query_pieces[:, key_value_head]]
    unnamed x86 -> x0, local copies, waits for them, and re-layouts: 11.3 us -> none
  transfers between devices with their start and end apart: 5 -> 0, of which waited for: 2 -> 0; matrix products, arithmetic and copies ran while one was open for 17% -> 0% of each run, Pallas kernels for 0% -> 0%
where the time goes in v1:
time: 70 us; the launch traced here: 69 us
  Pallas kernels  67.1 us (96%)
  between operations  1.94 us (3%)
    pallas_call x1, Pallas kernels, on_device(): pl.pallas_call(kernel, out_shape=results, in_specs=[smem] * 2 + [anywhere...  64.9 us
    pallas_call x1, Pallas kernels, on_device(): pl.pallas_call(finish_kernel, out_shape=results, in_specs=[anywhere] * 5,...  2.23 us

profile of v1, /device:TPU:6, one launch (start us, length us, event | category | flops | bytes accessed | tf_op | source)
XLA Modules:
  0.0 69.0 jit_solution(6115997593311238043)
XLA Ops:
  1.9 64.9 %whole.1 = (bf16[1,128,4096]{2,1,0:T(8,128)(2,1)}, f32[16,512]{1,0:T(8,128)}, f32[16,512]{1,0:T(8,128)}, f32[16,512]{1,0:T(8,128)}, f32[16,16]{1,0:T(8,128)}) custom-call(f32[1]{0:T(128)S(6)} %copy.20.advantages, s32[1]{0:T(128)S(6)} %copy.21.lengths, bf16[1,128,4096]{2,1,0:T(8,128)(2,1)} %queries_h.1, bf16[1,128,4096]{2,1,0:T(8,128)(2,1)} %outputs_h.1, ...), custom_call_target="tpu_custom_call" | custom-call | tf_op jit(solution)/shard_map/whole/pallas_call | solution.py:485
  66.8 2.2 %finish.1 = (bf16[1,128,4096]{2,1,0:T(8,128)(2,1)}, f32[16,512]{1,0:T(8,128)}, f32[16,512]{1,0:T(8,128)}, f32[16,512]{1,0:T(8,128)}, f32[16,16]{1,0:T(8,128)}) custom-call(bf16[1,128,4096]{2,1,0:T(8,128)(2,1)} %get-tuple-element.10.refs_0_, f32[16,512]{1,0:T(8,128)} %get-tuple-element.11.refs_1_, f32[16,512]{1,0:T(8,128)} %get-tuple-element.12.refs_2_, ...), custom_call_target="tpu_custom_call" | custom-call | tf_op jit(solution)/shard_map/finish/pallas_call | solution.py:544

commit v2 on v1

--- a/solution.py
+++ b/solution.py
@@ -43,10 +43,10 @@
     return lax.rem(value + offset + count, count)
 
 
-LINE, AY, AX, CORE, STATES, TILES, MAPS, BACKS, SUMS = 0, 1, 2, 3, 5, 6, 7, 8, 9
-BX, BY, HALVES = 10, 16, 22
-FIRST, SECOND, LINES, PIECES = 26, 30, 34, 36
-SEMS = 38
+LINE, AY, AX, CORE, STATES, TILES, MAPS, BACKS, SUMS = 0, 3, 4, 5, 8, 9, 10, 11, 12
+BX, BY, HALVES = 13, 22, 25
+FIRST, SECOND, LINES, PIECES = 29, 33, 37, 39
+SEMS = 41
 
 
 def kernel(
@@ -61,6 +61,7 @@
 ):
     ctx, resp, x, q, zh, c, zl, y = place()
     other = 1 - c
+    yk, yg = lax.div(y, 2), lax.rem(y, 2)
     z = zh * ZL + zl
 
     xs = [(step(x, d, X) * GROUP + q, resp) for d in range(1, X)]
@@ -133,11 +134,15 @@
         for kind in range(2):
             for gl in range(2):
                 g = ch * 2 + gl
-                blocks[ch, kind * 2 + gl] = (keys, values)[kind][:, g * LANES:(g + 1) * LANES]
-    kv[:, y, c, x, zh] = blocks[:, y]
+                blocks[ch, kind, gl] = (keys, values)[kind][:, g * LANES:(g + 1) * LANES]
+    kv[0, :, :, c, x, zh] = blocks[0]
+    kv[1, yk, yg, c, x, zh] = blocks[1, yk, yg]
     pl.semaphore_wait(barrier, partners)
+    for gl in range(2):
+        for d in range(1, ZH):
+            send(blocks.at[0, :, gl], kv.at[0, :, gl, c, x, zh], zs[d - 1], LINE + gl)
     for d in range(1, ZH):
-        send(blocks.at[:, y], kv.at[:, y, c, x, zh], zs[d - 1], LINE)
+        send(blocks.at[1, yk, yg], kv.at[1, yk, yg, c, x, zh], zs[d - 1], LINE + 2)
 
     for i in range(2, 6):
         loads[i].wait()
@@ -160,12 +165,24 @@
     each(GROUP, lambda d: send(tiles_out.at[step(q, d, GROUP)], tiles_in.at[q], group(d), TILES))
     tiles_in[q] = tiles_out[q]
 
-    arrived(kv.at[:, y, c, x, 0:3], LINE)
+    for gl in range(2):
+        arrived(kv.at[0, :, gl, c, x, 0:3], LINE + gl)
+        here = kv.at[0, :, gl, c, x]
+        for d in range(1, 4):
+            send(here, here, xs[d - 1], BX + 3 * gl, BX + 3 * gl + d - 1)
+        send(here, here, partner, CORE + gl)
+    arrived(kv.at[1, yk, yg, c, x, 0:3], LINE + 2)
     for d in range(1, 4):
-        here = kv.at[:, y, c, x, 0:2]
+        here = kv.at[1, yk, yg, c, x, 0:2]
         send(here, here, ys[d - 1], AY)
-        here = kv.at[:, y, c, x, 2:4]
+        here = kv.at[1, yk, yg, c, x, 2:4]
         send(here, here, xs[d - 1], AX)
+
+    def send_state(d):
+        start = pl.multiple_of(step(resp, d, RESP) * CHANNELS + zh * LANES, LANES)
+        send(state_h.at[0, :, pl.ds(start, LANES)], state_in.at[d - 1], resps(d), STATES)
+
+    each(RESP, send_state)
 
     length = lengths[0]
     weight = advantages[0] * F32(TOKENS * lax.axis_size("ctx")) / length.astype(F32)
@@ -193,23 +210,6 @@
     own_t[...] = own[0] * LOG2E
     lax.fori_loop(0, 4, prepare, 0)
 
-    arrived(kv.at[:, 0:3, c, x, 0:2], AY)
-    arrived(kv.at[:, y, c, 0:3, 2:4], AX)
-    for ch in range(2):
-        by_x = kv.at[ch, :, c, x, 0:2]
-        by_y = kv.at[ch, y, c, :, 2:4]
-        for d in range(1, 4):
-            send(by_x, by_x, xs[d - 1], BX + 3 * ch, BX + 3 * ch + d - 1)
-            send(by_y, by_y, ys[d - 1], BY + 3 * ch, BY + 3 * ch + d - 1)
-        send(by_x, by_x, partner, CORE + ch)
-        send(by_y, by_y, partner, CORE + ch)
-
-    def send_state(d):
-        start = pl.multiple_of(step(resp, d, RESP) * CHANNELS + zh * LANES, LANES)
-        send(state_h.at[0, :, pl.ds(start, LANES)], state_in.at[d - 1], resps(d), STATES)
-
-    each(RESP, send_state)
-
     arrived(tiles_in.at[0:7], TILES)
     span_all = jnp.ones((8, LANES), F32)
     carry_all = jnp.zeros((8, LANES), F32)
@@ -222,14 +222,32 @@
         send(group_out, group_in.at[x], xs[d - 1], MAPS)
     group_in[x] = group_out[...]
 
-    def pass_on(ch):
+    def second_gather():
+        by_x = kv.at[1, :, :, c, x, 0:2]
+        by_y = kv.at[1, yk, yg, c, :, 2:4]
+        arrived(kv.at[1, 0, 0, c, 0:3, 0:2], AY)
+        arrived(kv.at[1, 0, 0, c, 0:3, 2:4], AX)
         for d in range(1, 4):
-            here = kv.at[ch, :, c, step(x, -d, X), 0:2]
-            arrived(here, BX + 3 * ch + d - 1)
-            send(here, here, partner, CORE + ch)
-            here = kv.at[ch, step(y, -d, Y), c, :, 2:4]
-            arrived(here, BY + 3 * ch + d - 1)
-            send(here, here, partner, CORE + ch)
+            send(by_x, by_x, xs[d - 1], BX + 6, BX + 6 + d - 1)
+            send(by_y, by_y, ys[d - 1], BY, BY + d - 1)
+        send(by_x, by_x, partner, CORE + 2)
+        send(by_y, by_y, partner, CORE + 2)
+
+    def pass_head(gl):
+        for d in range(1, 4):
+            here = kv.at[0, :, gl, c, step(x, -d, X)]
+            arrived(here, BX + 3 * gl + d - 1)
+            send(here, here, partner, CORE + gl)
+
+    def pass_chunk():
+        for d in range(1, 4):
+            here = kv.at[1, :, :, c, step(x, -d, X), 0:2]
+            arrived(here, BX + 6 + d - 1)
+            send(here, here, partner, CORE + 2)
+            from_y = step(y, -d, Y)
+            here = kv.at[1, lax.div(from_y, 2), lax.rem(from_y, 2), c, :, 2:4]
+            arrived(here, BY + d - 1)
+            send(here, here, partner, CORE + 2)
 
     def carry_back():
         for i in range(10, 13):
@@ -252,11 +270,11 @@
         return jnp.concatenate([ref[0, :, h * SIZE:(h + 1) * SIZE] for h in heads], axis=0)
 
     def keys_of(g):
-        return kv[g // 2, g % 2].reshape(KEYS, SIZE)
+        return kv[g // 2, 0, g % 2].reshape(KEYS, SIZE)
 
     def begin(pair):
         g = pair // 4
-        values_g = kv[g // 2, 2 + g % 2].reshape(KEYS, SIZE)
+        values_g = kv[g // 2, 1, g % 2].reshape(KEYS, SIZE)
         scores = lax.dot_general(keys_of(g), rows(queries, pair), NT, preferred_element_type=F32) * (SCALE * LOG2E)
         dprobs = lax.dot_general(values_g, rows(grads, pair), NT, preferred_element_type=F32)
         return scores, dprobs
@@ -339,9 +357,11 @@
             pieces[ch * Y + y] = summed
 
     loads[9].wait()
-    pass_on(0)
+    pass_head(0)
+    second_gather()
     lax.fori_loop(4, 8, prepare, 0)
-    arrived(kv.at[0, :, other], CORE)
+    pass_head(1)
+    arrived(kv.at[0, :, 0, other], CORE)
     begun = begin(0)
     for pair in range(HEADS // 2):
         g = pair // 4
@@ -349,9 +369,11 @@
             transposed = keys_of(g).T
             sums = (jnp.zeros((KEYS, SIZE), F32),) * 2
         if pair == 3:
-            pass_on(1)
+            arrived(kv.at[0, :, 1, other], CORE + 1)
+        if pair == 4:
+            pass_chunk()
         if pair == 7:
-            arrived(kv.at[1, :, other], CORE + 1)
+            arrived(kv.at[1, :, :, other], CORE + 2)
         ahead = begin(pair + 1) if pair + 1 < HEADS // 2 else None
         sums = end(pair, begun, transposed, sums)
         begun = ahead
@@ -398,15 +420,18 @@
     map_out[...] = square[...].T[0:16, 0:16]
     sum_line(1)
 
-    left(blocks.at[:, 0:3], LINE)
+    for gl in range(2):
+        left(kv.at[0, :, gl, c, x, 0:3], LINE + gl)
+        left(kv.at[0, :, gl, c, 0:3], BX + 3 * gl)
+        left(kv.at[0, :, gl, c], CORE + gl)
+    left(kv.at[1, 0, 0, c, x, 0:3], LINE + 2)
     left(tiles_out.at[0:7], TILES)
-    left(kv.at[:, 0:3, c, x, 0:2], AY)
-    left(kv.at[:, y, c, 0:3, 2:4], AX)
+    left(kv.at[1, 0, 0, c, 0:3, 0:2], AY)
+    left(kv.at[1, 0, 0, c, 0:3, 2:4], AX)
+    left(kv.at[1, :, :, c, 0:3, 0:2], BX + 6)
+    left(kv.at[0, :, 0, c, 0:3], BY)
+    left(kv.at[1, :, :, c], CORE + 2)
     left(state_in.at[0:15], STATES)
-    for ch in range(2):
-        left(kv.at[ch, :, c, 0:3, 0:2], BX + 3 * ch)
-        left(kv.at[ch, 0:3, c, :, 2:4], BY + 3 * ch)
-        left(kv.at[ch, :, c], CORE + ch)
     left(group_in.at[0:3], MAPS)
     left(back_out.at[0:7], BACKS)
     for g in range(KV_HEADS):
@@ -501,8 +526,8 @@
             pltpu.VMEM((BLOCK, STATE), F32),
             pltpu.VMEM((BLOCK, CHANNELS), BF16),
             pltpu.VMEM((STATE, LANES), BF16),
-            pltpu.VMEM((2, 4, BLOCK, LANES), BF16),
-            pltpu.VMEM((2, 4, CORES, X) + tile, BF16),
+            pltpu.VMEM((2, 2, 2, BLOCK, LANES), BF16),
+            pltpu.VMEM((2, 2, 2, CORES, X) + tile, BF16),
             pltpu.VMEM((HEADS, TOKENS), F32),
             pltpu.VMEM((HEADS, 8, TOKENS), F32),
             pltpu.VMEM((LANES, LANES), F32),

time: 70 us -> 68.9 us (0.984)
  Pallas kernels: 67.1 us -> 66.1 us
    pallas_call x1, Pallas kernels: 64.9 us -> 63.9 us  [on_device(): pl.pallas_call(kernel, out_shape=results, in_specs=[smem] * 2 + [anywhere...]
where the time goes in v2:
time: 68.9 us; the launch traced here: 68 us
  Pallas kernels  66.1 us (96%)
  between operations  1.94 us (3%)
    pallas_call x1, Pallas kernels, on_device(): pl.pallas_call(kernel, out_shape=results, in_specs=[smem] * 2 + [anywhere...  63.9 us
    pallas_call x1, Pallas kernels, on_device(): pl.pallas_call(finish_kernel, out_shape=results, in_specs=[anywhere] * 5,...  2.23 us

profile of v2, /device:TPU:6, one launch (start us, length us, event | category | flops | bytes accessed | tf_op | source)
XLA Modules:
  0.0 68.0 jit_solution(7289145176261300820)
XLA Ops:
  1.9 63.9 %whole.1 = (bf16[1,128,4096]{2,1,0:T(8,128)(2,1)}, f32[16,512]{1,0:T(8,128)}, f32[16,512]{1,0:T(8,128)}, f32[16,512]{1,0:T(8,128)}, f32[16,16]{1,0:T(8,128)}) custom-call(f32[1]{0:T(128)S(6)} %copy.20.advantages, s32[1]{0:T(128)S(6)} %copy.21.lengths, bf16[1,128,4096]{2,1,0:T(8,128)(2,1)} %queries_h.1, bf16[1,128,4096]{2,1,0:T(8,128)(2,1)} %outputs_h.1, ...), custom_call_target="tpu_custom_call" | custom-call | tf_op jit(solution)/shard_map/whole/pallas_call | solution.py:510
  65.8 2.2 %finish.1 = (bf16[1,128,4096]{2,1,0:T(8,128)(2,1)}, f32[16,512]{1,0:T(8,128)}, f32[16,512]{1,0:T(8,128)}, f32[16,512]{1,0:T(8,128)}, f32[16,16]{1,0:T(8,128)}) custom-call(bf16[1,128,4096]{2,1,0:T(8,128)(2,1)} %get-tuple-element.10.refs_0_, f32[16,512]{1,0:T(8,128)} %get-tuple-element.11.refs_1_, f32[16,512]{1,0:T(8,128)} %get-tuple-element.12.refs_2_, ...), custom_call_target="tpu_custom_call" | custom-call | tf_op jit(solution)/shard_map/finish/pallas_call | solution.py:569

commit v3 on v2

--- a/solution.py
+++ b/solution.py
@@ -208,7 +208,7 @@
     for i in range(6, 9):
         loads[i].wait()
     own_t[...] = own[0] * LOG2E
-    lax.fori_loop(0, 4, prepare, 0)
+    lax.fori_loop(0, 6, prepare, 0)
 
     arrived(tiles_in.at[0:7], TILES)
     span_all = jnp.ones((8, LANES), F32)
@@ -287,15 +287,18 @@
         top = jnp.maximum(jnp.max(scores, axis=0, keepdims=True), own2)
         powers = jnp.exp2(scores - top)
         total = jnp.sum(powers, axis=0, keepdims=True) + jnp.exp2(own2 - top)
-        probs = powers * (1.0 / total)
-        dscores = (probs * (dprobs - inner)).astype(BF16)
+        tiled = (KEYS // BLOCK, BLOCK, 2 * SIZE)
+        share = jnp.broadcast_to(1.0 / total, (BLOCK, 2 * SIZE)).astype(BF16)
+        probs = powers.astype(BF16).reshape(tiled) * share[None]
+        dscores = (probs * (dprobs - inner).astype(BF16).reshape(tiled)).reshape(KEYS, 2 * SIZE)
+        probs = probs.reshape(KEYS, 2 * SIZE)
         query_t = jnp.dot(transposed, dscores, preferred_element_type=F32) * SCALE
         for i in range(2):
             part = query_t[:, i * SIZE:(i + 1) * SIZE].T.astype(BF16)
             query_out[0, :, (h + i) * SIZE:(h + i + 1) * SIZE] = part
         return (
             sums[0] + jnp.dot(dscores, rows(queries, pair), preferred_element_type=F32),
-            sums[1] + jnp.dot(probs.astype(BF16), rows(grads, pair), preferred_element_type=F32),
+            sums[1] + jnp.dot(probs, rows(grads, pair), preferred_element_type=F32),
         )
 
     def ship(g, sums):
@@ -351,7 +354,7 @@
         def _():
             line_in[z] = lines[ch, zh]
             arrived(line_in.at[0:15], LINES + ch)
-            summed = jnp.sum(line_in[...].astype(F32), axis=0)
+            summed = jnp.sum(line_in[...].astype(F32), axis=0).astype(BF16)
             piece[...] = summed
             each(RESP, lambda d: send(piece, pieces.at[ch * Y + y], resps(d), PIECES + ch))
             pieces[ch * Y + y] = summed
@@ -359,7 +362,7 @@
     loads[9].wait()
     pass_head(0)
     second_gather()
-    lax.fori_loop(4, 8, prepare, 0)
+    lax.fori_loop(6, 8, prepare, 0)
     pass_head(1)
     arrived(kv.at[0, :, 0, other], CORE)
     begun = begin(0)
@@ -415,10 +418,10 @@
     each(RESP, lambda d: send(db_out, db_in.at[d - 1], resps(d), SUMS))
     to_lines(1)
     sum_line(0)
+    sum_line(1)
     arrived(db_in.at[0:15], SUMS)
     square[0:STATE, :] = db_out[...] + jnp.sum(db_in[...], axis=0)
     map_out[...] = square[...].T[0:16, 0:16]
-    sum_line(1)
 
     for gl in range(2):
         left(kv.at[0, :, gl, c, x, 0:3], LINE + gl)
@@ -446,7 +449,7 @@
         @pl.when(zl == 1 + ch)
         def _():
             left(line_in.at[0:3], LINES + ch)
-            left(db_in.at[0:15], PIECES + ch)
+            left(line_in.at[0:15], PIECES + ch)
 
         @pl.when(zl != 1 + ch)
         def _():
@@ -467,8 +470,8 @@
 
         for gl in range(2):
             cols = slice((ch * 2 + gl) * LANES, (ch * 2 + gl + 1) * LANES)
-            key_grad[:, cols] = pieces[ch * Y + gl] * SCALE
-            value_grad[:, cols] = pieces[ch * Y + 2 + gl]
+            key_grad[:, cols] = pieces[ch * Y + gl].astype(F32) * SCALE
+            value_grad[:, cols] = pieces[ch * Y + 2 + gl].astype(F32)
 
 
 def finish_kernel(*refs):
@@ -550,8 +553,8 @@
             pltpu.VMEM((2, 2, 3) + half, BF16),
             pltpu.VMEM((2,) + tile, BF16),
             pltpu.VMEM((Z, BLOCK, LANES), BF16),
-            pltpu.VMEM((BLOCK, LANES), F32),
-            pltpu.VMEM((2 * Y, BLOCK, LANES), F32),
+            pltpu.VMEM((BLOCK, LANES), BF16),
+            pltpu.VMEM((2 * Y, BLOCK, LANES), BF16),
             pltpu.VMEM(wide, BF16),
             pltpu.SemaphoreType.DMA((13,)),
             pltpu.SemaphoreType.DMA((KV_HEADS,)),

time: 68.9 us -> 68.7 us (level)
  no operation moved by 1% of the time
where the time goes in v3:
time: 68.7 us; the launch traced here: 67.8 us
  Pallas kernels  65.8 us (96%)
  between operations  1.94 us (3%)
    pallas_call x1, Pallas kernels, on_device(): pl.pallas_call(kernel, out_shape=results, in_specs=[smem] * 2 + [anywhere...  63.6 us
    pallas_call x1, Pallas kernels, on_device(): pl.pallas_call(finish_kernel, out_shape=results, in_specs=[anywhere] * 5,...  2.23 us

profile of v3, /device:TPU:6, one launch (start us, length us, event | category | flops | bytes accessed | tf_op | source)
XLA Modules:
  0.0 67.8 jit_solution(3743484054711520161)
XLA Ops:
  1.9 63.6 %whole.1 = (bf16[1,128,4096]{2,1,0:T(8,128)(2,1)}, f32[16,512]{1,0:T(8,128)}, f32[16,512]{1,0:T(8,128)}, f32[16,512]{1,0:T(8,128)}, f32[16,16]{1,0:T(8,128)}) custom-call(f32[1]{0:T(128)S(6)} %copy.20.advantages, s32[1]{0:T(128)S(6)} %copy.21.lengths, bf16[1,128,4096]{2,1,0:T(8,128)(2,1)} %queries_h.1, bf16[1,128,4096]{2,1,0:T(8,128)(2,1)} %outputs_h.1, ...), custom_call_target="tpu_custom_call" | custom-call | tf_op jit(solution)/shard_map/whole/pallas_call | solution.py:513
  65.5 2.2 %finish.1 = (bf16[1,128,4096]{2,1,0:T(8,128)(2,1)}, f32[16,512]{1,0:T(8,128)}, f32[16,512]{1,0:T(8,128)}, f32[16,512]{1,0:T(8,128)}, f32[16,16]{1,0:T(8,128)}) custom-call(bf16[1,128,4096]{2,1,0:T(8,128)(2,1)} %get-tuple-element.10.refs_0_, f32[16,512]{1,0:T(8,128)} %get-tuple-element.11.refs_1_, f32[16,512]{1,0:T(8,128)} %get-tuple-element.12.refs_2_, ...), custom_call_target="tpu_custom_call" | custom-call | tf_op jit(solution)/shard_map/finish/pallas_call | solution.py:572

commit v4 on v3

--- a/solution.py
+++ b/solution.py
@@ -287,18 +287,15 @@
         top = jnp.maximum(jnp.max(scores, axis=0, keepdims=True), own2)
         powers = jnp.exp2(scores - top)
         total = jnp.sum(powers, axis=0, keepdims=True) + jnp.exp2(own2 - top)
-        tiled = (KEYS // BLOCK, BLOCK, 2 * SIZE)
-        share = jnp.broadcast_to(1.0 / total, (BLOCK, 2 * SIZE)).astype(BF16)
-        probs = powers.astype(BF16).reshape(tiled) * share[None]
-        dscores = (probs * (dprobs - inner).astype(BF16).reshape(tiled)).reshape(KEYS, 2 * SIZE)
-        probs = probs.reshape(KEYS, 2 * SIZE)
+        probs = powers * (1.0 / total)
+        dscores = (probs * (dprobs - inner)).astype(BF16)
         query_t = jnp.dot(transposed, dscores, preferred_element_type=F32) * SCALE
         for i in range(2):
             part = query_t[:, i * SIZE:(i + 1) * SIZE].T.astype(BF16)
             query_out[0, :, (h + i) * SIZE:(h + i + 1) * SIZE] = part
         return (
             sums[0] + jnp.dot(dscores, rows(queries, pair), preferred_element_type=F32),
-            sums[1] + jnp.dot(probs, rows(grads, pair), preferred_element_type=F32),
+            sums[1] + jnp.dot(probs.astype(BF16), rows(grads, pair), preferred_element_type=F32),
         )
 
     def ship(g, sums):
@@ -307,6 +304,28 @@
             partial[ch, kind, gl] = sums[kind].astype(BF16).reshape(partial.shape[3:])
         send(partial.at[ch, :, gl, other], core_in.at[ch, :, gl], partner, HALVES + g)
         store(g).start()
+
+    def finish_scan():
+        arrived(back_in.at[0:7], BACKS)
+        square_in[...] = jnp.zeros_like(square_in)
+        square_in[0:16, 0:16] = input_map[...]
+        in_t = square_in[...].T
+        taken = steps * mamba_in[...].astype(F32)
+        carry = jnp.concatenate(
+            [jnp.concatenate([back_in[kt * 2 + nh] for kt in range(4)], axis=1) for nh in range(2)], axis=0
+        )
+        lane = lax.broadcasted_iota(jnp.int32, (STATE, LANES), 1)
+        db = jnp.zeros((STATE, LANES), F32)
+        for t in range(BLOCK - 1, -1, -1):
+            adjoint = out_t[0:STATE, t:t + 1] * dy[t:t + 1] + carry
+            total = jnp.sum(in_t[0:STATE, t:t + 1] * adjoint, axis=0, keepdims=True)
+            mamba_out[t:t + 1, :] = steps[t:t + 1] * total
+            term = adjoint * taken[t:t + 1]
+            term = (term[:, 0:128] + term[:, 128:256]) + (term[:, 256:384] + term[:, 384:512])
+            db = jnp.where(lane == t, jnp.sum(term, axis=1, keepdims=True), db)
+            carry = decays[t] * adjoint
+        db_out[...] = db
+        each(RESP, lambda d: send(db_out, db_in.at[d - 1], resps(d), SUMS))
 
     def join(g):
         ch, gl = g // 2, g % 2
@@ -388,34 +407,14 @@
             if g == 2:
                 join(1)
                 first_hop(0)
+                finish_scan()
     join(2)
     second_hop(0)
     join(3)
     first_hop(1)
     to_lines(0)
 
-    arrived(back_in.at[0:7], BACKS)
-    square_in[...] = jnp.zeros_like(square_in)
-    square_in[0:16, 0:16] = input_map[...]
-    in_t = square_in[...].T
-    taken = steps * mamba_in[...].astype(F32)
-    carry = jnp.concatenate(
-        [jnp.concatenate([back_in[kt * 2 + nh] for kt in range(4)], axis=1) for nh in range(2)], axis=0
-    )
-    lane = lax.broadcasted_iota(jnp.int32, (STATE, LANES), 1)
-    db = jnp.zeros((STATE, LANES), F32)
-    for t in range(BLOCK - 1, -1, -1):
-        adjoint = out_t[0:STATE, t:t + 1] * dy[t:t + 1] + carry
-        total = jnp.sum(in_t[0:STATE, t:t + 1] * adjoint, axis=0, keepdims=True)
-        mamba_out[t:t + 1, :] = steps[t:t + 1] * total
-        term = adjoint * taken[t:t + 1]
-        term = (term[:, 0:128] + term[:, 128:256]) + (term[:, 256:384] + term[:, 384:512])
-        db = jnp.where(lane == t, jnp.sum(term, axis=1, keepdims=True), db)
-        carry = decays[t] * adjoint
-    db_out[...] = db
-
     second_hop(1)
-    each(RESP, lambda d: send(db_out, db_in.at[d - 1], resps(d), SUMS))
     to_lines(1)
     sum_line(0)
     sum_line(1)

time: 68.7 us -> 70.7 us (1.029)
  Pallas kernels: 65.8 us -> 68.3 us
    pallas_call x1, Pallas kernels: 63.6 us -> 66.1 us  [on_device(): pl.pallas_call(kernel, out_shape=results, in_specs=[smem] * 2 + [anywhere...]
where the time goes in v4:
time: 70.7 us; the launch traced here: 70.3 us
  Pallas kernels  68.3 us (97%)
  between operations  1.94 us (3%)
    pallas_call x1, Pallas kernels, on_device(): pl.pallas_call(kernel, out_shape=results, in_specs=[smem] * 2 + [anywhere...  66.1 us
    pallas_call x1, Pallas kernels, on_device(): pl.pallas_call(finish_kernel, out_shape=results, in_specs=[anywhere] * 5,...  2.23 us

profile of v4, /device:TPU:6, one launch (start us, length us, event | category | flops | bytes accessed | tf_op | source)
XLA Modules:
  0.0 70.3 jit_solution(10990637186226734450)
XLA Ops:
  1.9 66.1 %whole.1 = (bf16[1,128,4096]{2,1,0:T(8,128)(2,1)}, f32[16,512]{1,0:T(8,128)}, f32[16,512]{1,0:T(8,128)}, f32[16,512]{1,0:T(8,128)}, f32[16,16]{1,0:T(8,128)}) custom-call(f32[1]{0:T(128)S(6)} %copy.20.advantages, s32[1]{0:T(128)S(6)} %copy.21.lengths, bf16[1,128,4096]{2,1,0:T(8,128)(2,1)} %queries_h.1, bf16[1,128,4096]{2,1,0:T(8,128)(2,1)} %outputs_h.1, ...), custom_call_target="tpu_custom_call" | custom-call | tf_op jit(solution)/shard_map/whole/pallas_call | solution.py:512
  68.1 2.2 %finish.1 = (bf16[1,128,4096]{2,1,0:T(8,128)(2,1)}, f32[16,512]{1,0:T(8,128)}, f32[16,512]{1,0:T(8,128)}, f32[16,512]{1,0:T(8,128)}, f32[16,16]{1,0:T(8,128)}) custom-call(bf16[1,128,4096]{2,1,0:T(8,128)(2,1)} %get-tuple-element.10.refs_0_, f32[16,512]{1,0:T(8,128)} %get-tuple-element.11.refs_1_, f32[16,512]{1,0:T(8,128)} %get-tuple-element.12.refs_2_, ...), custom_call_target="tpu_custom_call" | custom-call | tf_op jit(solution)/shard_map/finish/pallas_call | solution.py:571

commit v5 on v3

--- a/solution.py
+++ b/solution.py
@@ -188,21 +188,20 @@
     weight = advantages[0] * F32(TOKENS * lax.axis_size("ctx")) / length.astype(F32)
     position = ctx * TOKENS + lax.broadcasted_iota(jnp.int32, (TOKENS, 1), 0)
     token_weight = jnp.where(position < length, weight, F32(0.0))
-    ones = jnp.ones((8, SIZE), BF16)
+    ones = jnp.ones((8, 2 * SIZE), BF16)
 
     def prepare(quad, carry):
-        for i in range(4):
-            h = quad * 4 + i
-            cols = pl.ds(pl.multiple_of(h * SIZE, SIZE), SIZE)
+        for i in range(2):
+            pair = quad * 2 + i
+            cols = pl.ds(pl.multiple_of(pair * 2 * SIZE, 2 * SIZE), 2 * SIZE)
             scaled = (grads[0, :, cols].astype(F32) * token_weight).astype(BF16)
             grads[0, :, cols] = scaled
             product = scaled.astype(F32) * outputs[0, :, cols].astype(F32)
+            product = jnp.concatenate([product[:, 0:SIZE], product[:, SIZE:2 * SIZE]], axis=0)
             high = product.astype(BF16)
             low = (product - high.astype(F32)).astype(BF16)
-            inners[h] = (
-                lax.dot_general(ones, high, NT, preferred_element_type=F32)
-                + lax.dot_general(ones, low, NT, preferred_element_type=F32)
-            )
+            both = jnp.concatenate([high, low], axis=1)
+            inners[pair] = lax.dot_general(ones, both, NT, preferred_element_type=F32)
         return carry
 
     for i in range(6, 9):
@@ -282,23 +281,20 @@
     def end(pair, begun, transposed, sums):
         scores, dprobs = begun
         h = 2 * pair
-        inner = jnp.concatenate([inners[h, 0:1], inners[h + 1, 0:1]], axis=1)
+        inner = inners[pair, 0:1]
         own2 = jnp.concatenate([own_t[h:h + 1], own_t[h + 1:h + 2]], axis=1)
         top = jnp.maximum(jnp.max(scores, axis=0, keepdims=True), own2)
         powers = jnp.exp2(scores - top)
         total = jnp.sum(powers, axis=0, keepdims=True) + jnp.exp2(own2 - top)
-        tiled = (KEYS // BLOCK, BLOCK, 2 * SIZE)
-        share = jnp.broadcast_to(1.0 / total, (BLOCK, 2 * SIZE)).astype(BF16)
-        probs = powers.astype(BF16).reshape(tiled) * share[None]
-        dscores = (probs * (dprobs - inner).astype(BF16).reshape(tiled)).reshape(KEYS, 2 * SIZE)
-        probs = probs.reshape(KEYS, 2 * SIZE)
+        probs = powers * (1.0 / total)
+        dscores = (probs * (dprobs - inner)).astype(BF16)
         query_t = jnp.dot(transposed, dscores, preferred_element_type=F32) * SCALE
         for i in range(2):
             part = query_t[:, i * SIZE:(i + 1) * SIZE].T.astype(BF16)
             query_out[0, :, (h + i) * SIZE:(h + i + 1) * SIZE] = part
         return (
             sums[0] + jnp.dot(dscores, rows(queries, pair), preferred_element_type=F32),
-            sums[1] + jnp.dot(probs, rows(grads, pair), preferred_element_type=F32),
+            sums[1] + jnp.dot(probs.astype(BF16), rows(grads, pair), preferred_element_type=F32),
         )
 
     def ship(g, sums):
@@ -364,6 +360,7 @@
     second_gather()
     lax.fori_loop(6, 8, prepare, 0)
     pass_head(1)
+    carry_back()
     arrived(kv.at[0, :, 0, other], CORE)
     begun = begin(0)
     for pair in range(HEADS // 2):
@@ -384,7 +381,6 @@
             ship(g, sums)
             if g == 1:
                 join(0)
-                carry_back()
             if g == 2:
                 join(1)
                 first_hop(0)
@@ -532,7 +528,7 @@
             pltpu.VMEM((2, 2, 2, BLOCK, LANES), BF16),
             pltpu.VMEM((2, 2, 2, CORES, X) + tile, BF16),
             pltpu.VMEM((HEADS, TOKENS), F32),
-            pltpu.VMEM((HEADS, 8, TOKENS), F32),
+            pltpu.VMEM((HEADS // 2, 8, 2 * TOKENS), F32),
             pltpu.VMEM((LANES, LANES), F32),
             pltpu.VMEM((LANES, LANES), F32),
             pltpu.VMEM((BLOCK, STATE, CHANNELS), F32),

time: 68.7 us -> 68.6 us (level)
  no operation moved by 1% of the time
where the time goes in v5:
time: 68.6 us; the launch traced here: 67.6 us
  Pallas kernels  65.7 us (96%)
  between operations  1.94 us (3%)
    pallas_call x1, Pallas kernels, on_device(): pl.pallas_call(kernel, out_shape=results, in_specs=[smem] * 2 + [anywhere...  63.4 us
    pallas_call x1, Pallas kernels, on_device(): pl.pallas_call(finish_kernel, out_shape=results, in_specs=[anywhere] * 5,...  2.23 us

profile of v5, /device:TPU:6, one launch (start us, length us, event | category | flops | bytes accessed | tf_op | source)
XLA Modules:
  0.0 67.6 jit_solution(13789521704152745996)
XLA Ops:
  1.9 63.4 %whole.1 = (bf16[1,128,4096]{2,1,0:T(8,128)(2,1)}, f32[16,512]{1,0:T(8,128)}, f32[16,512]{1,0:T(8,128)}, f32[16,512]{1,0:T(8,128)}, f32[16,16]{1,0:T(8,128)}) custom-call(f32[1]{0:T(128)S(6)} %copy.20.advantages, s32[1]{0:T(128)S(6)} %copy.21.lengths, bf16[1,128,4096]{2,1,0:T(8,128)(2,1)} %queries_h.1, bf16[1,128,4096]{2,1,0:T(8,128)(2,1)} %outputs_h.1, ...), custom_call_target="tpu_custom_call" | custom-call | tf_op jit(solution)/shard_map/whole/pallas_call | solution.py:509
  65.4 2.2 %finish.1 = (bf16[1,128,4096]{2,1,0:T(8,128)(2,1)}, f32[16,512]{1,0:T(8,128)}, f32[16,512]{1,0:T(8,128)}, f32[16,512]{1,0:T(8,128)}, f32[16,16]{1,0:T(8,128)}) custom-call(bf16[1,128,4096]{2,1,0:T(8,128)(2,1)} %get-tuple-element.10.refs_0_, f32[16,512]{1,0:T(8,128)} %get-tuple-element.11.refs_1_, f32[16,512]{1,0:T(8,128)} %get-tuple-element.12.refs_2_, ...), custom_call_target="tpu_custom_call" | custom-call | tf_op jit(solution)/shard_map/finish/pallas_call | solution.py:568

commit v6 on v5

--- a/solution.py
+++ b/solution.py
@@ -43,6 +43,7 @@
     return lax.rem(value + offset + count, count)
 
 
+FAR_FIRST, FAR_LAST = (2, 1, 3), (1, 3, 2)
 LINE, AY, AX, CORE, STATES, TILES, MAPS, BACKS, SUMS = 0, 3, 4, 5, 8, 9, 10, 11, 12
 BX, BY, HALVES = 13, 22, 25
 FIRST, SECOND, LINES, PIECES = 29, 33, 37, 39
@@ -89,7 +90,7 @@
         (mamba_in_h, mamba_in), (input_map_h, input_map), (state_h.at[0, :, pl.ds(mine, LANES)], state_own),
     ]
     loads = [pltpu.make_async_copy(src, dst, load_sem.at[i]) for i, (src, dst) in enumerate(loads)]
-    for load in loads:
+    for load in loads[0:2]:
         load.start()
     wide = PER_KV * SIZE
 
@@ -109,6 +110,8 @@
     for j in range(1, ZL):
         each(ZH, lambda d: greet((x * GROUP + step(zh, d, ZH) * CORES + c, step(zl, j, ZL) * Y + y)))
     partners = 3 + 7 + 15 + 9
+    for load in loads[2:]:
+        load.start()
 
     def send(src, dst, target, sem, recv=None):
         pltpu.make_async_remote_copy(
@@ -139,9 +142,9 @@
     kv[1, yk, yg, c, x, zh] = blocks[1, yk, yg]
     pl.semaphore_wait(barrier, partners)
     for gl in range(2):
-        for d in range(1, ZH):
+        for d in FAR_FIRST:
             send(blocks.at[0, :, gl], kv.at[0, :, gl, c, x, zh], zs[d - 1], LINE + gl)
-    for d in range(1, ZH):
+    for d in FAR_FIRST:
         send(blocks.at[1, yk, yg], kv.at[1, yk, yg, c, x, zh], zs[d - 1], LINE + 2)
 
     for i in range(2, 6):
@@ -168,11 +171,11 @@
     for gl in range(2):
         arrived(kv.at[0, :, gl, c, x, 0:3], LINE + gl)
         here = kv.at[0, :, gl, c, x]
-        for d in range(1, 4):
+        for d in FAR_FIRST:
             send(here, here, xs[d - 1], BX + 3 * gl, BX + 3 * gl + d - 1)
         send(here, here, partner, CORE + gl)
     arrived(kv.at[1, yk, yg, c, x, 0:3], LINE + 2)
-    for d in range(1, 4):
+    for d in FAR_FIRST:
         here = kv.at[1, yk, yg, c, x, 0:2]
         send(here, here, ys[d - 1], AY)
         here = kv.at[1, yk, yg, c, x, 2:4]
@@ -226,20 +229,20 @@
         by_y = kv.at[1, yk, yg, c, :, 2:4]
         arrived(kv.at[1, 0, 0, c, 0:3, 0:2], AY)
         arrived(kv.at[1, 0, 0, c, 0:3, 2:4], AX)
-        for d in range(1, 4):
+        for d in FAR_FIRST:
             send(by_x, by_x, xs[d - 1], BX + 6, BX + 6 + d - 1)
             send(by_y, by_y, ys[d - 1], BY, BY + d - 1)
         send(by_x, by_x, partner, CORE + 2)
         send(by_y, by_y, partner, CORE + 2)
 
     def pass_head(gl):
-        for d in range(1, 4):
+        for d in FAR_LAST:
             here = kv.at[0, :, gl, c, step(x, -d, X)]
             arrived(here, BX + 3 * gl + d - 1)
             send(here, here, partner, CORE + gl)
 
     def pass_chunk():
-        for d in range(1, 4):
+        for d in FAR_LAST:
             here = kv.at[1, :, :, c, step(x, -d, X), 0:2]
             arrived(here, BX + 6 + d - 1)
             send(here, here, partner, CORE + 2)
@@ -313,7 +316,7 @@
             ).astype(BF16)
 
     def first_hop(ch):
-        for d in range(1, 4):
+        for d in FAR_FIRST:
             send(pairs.at[ch, :, step(x, d, X), 0:2], first_in.at[ch, 0, d - 1], xs[d - 1], FIRST + 2 * ch)
             send(pairs.at[ch, step(y, d, Y), :, 2:4], first_in.at[ch, 1, d - 1], ys[d - 1], FIRST + 2 * ch + 1)
 
@@ -325,7 +328,7 @@
             for d in range(3):
                 total = total + first_in[ch, axis, d].astype(F32)
             firsts[ch, axis] = total.astype(BF16)
-            for d in range(1, 4):
+            for d in FAR_FIRST:
                 to = step(y, d, Y) if axis == 0 else step(x, d, X)
                 target = (ys if axis == 0 else xs)[d - 1]
                 send(firsts.at[ch, axis, to], second_in.at[ch, axis, d - 1], target, SECOND + 2 * ch + axis)
@@ -474,10 +477,11 @@
     given, results, held = refs[0:5], refs[5:10], refs[10:15]
     sem_in, sem_out = refs[15], refs[16]
     part = (given[0].at[0], held[0].at[0], results[0].at[0])
-    moves = [(given[i], held[i], results[i]) for i in range(1, 5)]
+    moves = []
     for i in range(8):
         rows = slice(i * BLOCK, (i + 1) * BLOCK)
         moves.append(tuple(ref.at[rows] for ref in part))
+    moves += [(given[i], held[i], results[i]) for i in range(1, 5)]
     copies_in = [pltpu.make_async_copy(src, mid, sem_in.at[i]) for i, (src, mid, _) in enumerate(moves)]
     copies_out = [pltpu.make_async_copy(mid, dst, sem_out.at[i]) for i, (_, mid, dst) in enumerate(moves)]
     for copy in copies_in:

time: 68.6 us -> 68 us (level)
  no operation moved by 1% of the time
where the time goes in v6:
time: 68 us; the launch traced here: 67.1 us
  Pallas kernels  65.2 us (96%)
  between operations  1.94 us (3%)
    pallas_call x1, Pallas kernels, on_device(): pl.pallas_call(kernel, out_shape=results, in_specs=[smem] * 2 + [anywhere...  63 us
    pallas_call x1, Pallas kernels, on_device(): pl.pallas_call(finish_kernel, out_shape=results, in_specs=[anywhere] * 5,...  2.19 us

profile of v6, /device:TPU:6, one launch (start us, length us, event | category | flops | bytes accessed | tf_op | source)
XLA Modules:
  0.0 67.1 jit_solution(7601773590221334788)
XLA Ops:
  1.9 63.0 %whole.1 = (bf16[1,128,4096]{2,1,0:T(8,128)(2,1)}, f32[16,512]{1,0:T(8,128)}, f32[16,512]{1,0:T(8,128)}, f32[16,512]{1,0:T(8,128)}, f32[16,16]{1,0:T(8,128)}) custom-call(f32[1]{0:T(128)S(6)} %copy.20.advantages, s32[1]{0:T(128)S(6)} %copy.21.lengths, bf16[1,128,4096]{2,1,0:T(8,128)(2,1)} %queries_h.1, bf16[1,128,4096]{2,1,0:T(8,128)(2,1)} %outputs_h.1, ...), custom_call_target="tpu_custom_call" | custom-call | tf_op jit(solution)/shard_map/whole/pallas_call | solution.py:513
  65.0 2.2 %finish.1 = (bf16[1,128,4096]{2,1,0:T(8,128)(2,1)}, f32[16,512]{1,0:T(8,128)}, f32[16,512]{1,0:T(8,128)}, f32[16,512]{1,0:T(8,128)}, f32[16,16]{1,0:T(8,128)}) custom-call(bf16[1,128,4096]{2,1,0:T(8,128)(2,1)} %get-tuple-element.10.refs_0_, f32[16,512]{1,0:T(8,128)} %get-tuple-element.11.refs_1_, f32[16,512]{1,0:T(8,128)} %get-tuple-element.12.refs_2_, ...), custom_call_target="tpu_custom_call" | custom-call | tf_op jit(solution)/shard_map/finish/pallas_call | solution.py:572
